TPU v7x, 32 devices: a whole 2x2x4 slice. The times are simulated.
32 devices in a mesh: cast: 8 (over z, x), width: 4 (over y, core).
Axes of the slice: x: 2, y: 2, z: 4, core: 2. Of those that a mesh axis runs over, the one named last changes fastest.
Arguments:
- stored_caloric_content: float32 [64, 64, 512], P(None, 'cast', 'width'), may hold values from -6 to 6
- zones: int32 [2, 64, 512], P(None, 'cast', 'width'), may hold values from 0 to 9
- spray_coef: float32 [10], replicated, may hold values from 0.2 to 5
Outputs:
- new_enthalpy: float32 [64, 64, 512], P(None, 'cast', 'width')
All inputs are finite; a program needn't handle non-finite values.
Results may differ from a plain program's by a relative error of at most 0.0018.
Values sent between devices are 32-bit elements; how exact they have to be, the bound alone decides.
A program may use at most 64 MiB of HBM per device.

v0:
```python
import functools

import jax
import jax.numpy as jnp
from jax import lax
from jax.experimental import pallas as pl
from jax.experimental.pallas import tpu as pltpu
from jax.sharding import PartitionSpec as P

RELEASE = 0.4
MEDIUM = -2.0


def medium(x):
    t = jnp.tanh(x)
    hot = x - RELEASE * t
    cond = 1.5 - 0.5 * jnp.tanh(hot)
    return t, hot, cond


def lane_levels(ground, gl, gr, left, right):
    axis = ground.ndim - 1
    size = ground.shape[axis]
    lane = lax.broadcasted_iota(jnp.int32, ground.shape, axis)
    ends = left + right
    factors = []
    step = 1
    while step < size:
        w = 1.0 / (ground + gl + gr)
        al = gl * pltpu.roll(w, step, axis)
        ga = gr * pltpu.roll(w, size - step, axis)
        factors.append((al, ga))
        ground = (
            ground
            + al * pltpu.roll(ground, step, axis)
            + ga * pltpu.roll(ground, size - step, axis)
        )
        from_left = al * pltpu.roll(ends, step, axis)
        from_right = ga * pltpu.roll(ends, size - step, axis)
        if 2 * step < size:
            ends = ends + from_left + from_right
            gl = al * pltpu.roll(gl, step, axis)
            gr = ga * pltpu.roll(gr, size - step, axis)
        else:
            left = jnp.where(lane < step, ends, 0.0) + from_left
            right = jnp.where(lane >= step, ends, 0.0) + from_right
        step *= 2
    return ground, left, right, factors


def row_levels(ground, links, left, right, r):
    count = len(ground)
    zero = jnp.zeros_like(left)
    ground = list(ground)
    ground[0] = ground[0] + left
    ground[-1] = ground[-1] + right
    lefts = [left] + [zero] * (count - 1)
    rights = [zero] * (count - 1) + [right]
    step = 1
    while step < count:
        w = []
        for j in range(count):
            total = ground[j]
            if j >= step:
                total = total + links[j - step]
            if j + step < count:
                total = total + links[j]
            w.append(1.0 / total)
        new_ground, new_r = list(ground), list(r)
        new_left, new_right = list(lefts), list(rights)
        new_links = [None] * count
        for j in range(count):
            if j >= step:
                al = links[j - step] * w[j - step]
                new_ground[j] = new_ground[j] + al * ground[j - step]
                new_r[j] = new_r[j] + al * r[j - step]
                if j - step < step:
                    new_left[j] = new_left[j] + al * lefts[j - step]
                if j >= 2 * step:
                    new_links[j - 2 * step] = al * links[j - 2 * step]
            if j + step < count:
                ga = links[j] * w[j + step]
                new_ground[j] = new_ground[j] + ga * ground[j + step]
                new_r[j] = new_r[j] + ga * r[j + step]
                if j + step >= count - step:
                    new_right[j] = new_right[j] + ga * rights[j + step]
        ground, r, lefts, rights, links = new_ground, new_r, new_left, new_right, new_links
        step *= 2
    w = [1.0 / g for g in ground]
    return [[a * b for a, b in zip(v, w)] for v in (r, lefts, rights)]


def apply_level(r, al, ga, step, axis):
    size = r.shape[axis]
    return r + al * pltpu.roll(r, step, axis) + ga * pltpu.roll(r, size - step, axis)


def chain_coefs(a1, a2, b1, b2):
    out = []
    e1 = None
    for i in range(len(a1)):
        if e1 is None:
            c, be = None, None
            f2 = a2[i]
            e1 = b2[i]
        else:
            c = 1.0 / (1.0 - a1[i] * e1)
            be = b1[i] * e1
            f2 = c * a2[i]
            e1 = be * f2 + b2[i]
        out.append((c, be, f2, e1))
    return out


def chain_values(a0, b0, a1, b1, coefs):
    n = len(a0)
    f0s, e0s = [], []
    e0 = None
    for i in range(n):
        c, be, f2, e1 = coefs[i]
        if e0 is None:
            f0 = a0[i]
            e0 = b0[i]
        else:
            f0 = c * (a0[i] + a1[i] * e0)
            e0 = b0[i] + b1[i] * e0 + be * f0
        f0s.append(f0)
        e0s.append(e0)
    first, last = [None] * n, [None] * n
    first[n - 1], last[n - 1] = f0s[n - 1], e0s[n - 1]
    for i in range(n - 2, -1, -1):
        _, _, f2, e1 = coefs[i]
        first[i] = f0s[i] + f2 * first[i + 1]
        last[i] = e0s[i] + e1 * first[i + 1]
    return first, last


def kernel(
    n, nw, x_hbm, zones_hbm, coef_ref, out_ref,
    x_ref, zones_ref, T, K, S, U, SX, WL, WR, Y, PP, Q, AL, GA, WW, WP, WQ, DX, D, M, V,
    rows_out, rows_lo, rows_hi, cols_out, cols_lo, cols_hi,
    cs, cr, xs, xr, wc, wv,
    in_sem, halo_send, halo_recv, a_send, a_recv, b_send, b_recv, c_send, c_recv, d_send, d_recv,
):
    depth, rows, lanes = x_ref.shape
    pz = depth // n
    bz = SX.shape[2]
    nb = depth // bz
    per = bz // pz
    me = lax.axis_index("cast")
    mw = lax.axis_index("width")
    f32 = jnp.float32

    x_copy = pltpu.make_async_copy(x_hbm, x_ref, in_sem.at[0])
    zones_copy = pltpu.make_async_copy(zones_hbm, zones_ref, in_sem.at[1])
    x_copy.start()
    zones_copy.start()

    barrier = pltpu.get_barrier_semaphore()
    for k in range(1, n):
        pl.semaphore_signal(barrier, inc=1, device_id={"cast": lax.rem(me + k, n)})
    for k in range(1, nw):
        pl.semaphore_signal(barrier, inc=1, device_id={"width": lax.rem(mw + k, nw)})

    lane2 = lax.broadcasted_iota(jnp.int32, (bz, lanes), 1)
    lane3 = lax.broadcasted_iota(jnp.int32, (rows, bz, lanes), 2)
    zero = jnp.zeros((bz, lanes), f32)
    cast_lo = (me > 0).astype(f32)
    cast_hi = (me < n - 1).astype(f32)
    width_lo = (mw > 0).astype(f32)
    width_hi = (mw < nw - 1).astype(f32)

    def pack(v, b):
        acc = zero
        for j in range(rows):
            acc = jnp.where(lane2 // 2 == j, pltpu.roll(v[j], 2 * j + 1, 1), acc)
        return pltpu.roll(acc, b * (2 * rows), 1)

    def spread(p, b, odd):
        q = pltpu.roll(p, lax.rem(lanes - b * (2 * rows), lanes), 1)
        return [
            jnp.broadcast_to(q[:, 2 * j + odd : 2 * j + odd + 1], (bz, lanes))
            for j in range(rows)
        ]

    def by_rows(ref, start):
        return [ref[pl.ds(start, bz), j, :] for j in range(rows)]

    x_copy.wait()
    rows_out[0] = x_ref[:, 0, :]
    rows_out[1] = x_ref[:, rows - 1, :]
    cols_out[...] = lax.fori_loop(
        0, nb, lambda b, acc: acc + pack(by_rows(x_ref, b * bz), b), zero
    )

    @pl.when(me == 0)
    def _():
        rows_lo[...] = jnp.zeros_like(rows_lo)

    @pl.when(me == n - 1)
    def _():
        rows_hi[...] = jnp.zeros_like(rows_hi)

    @pl.when(mw == 0)
    def _():
        cols_lo[...] = jnp.zeros_like(cols_lo)

    @pl.when(mw == nw - 1)
    def _():
        cols_hi[...] = jnp.zeros_like(cols_hi)

    def remote(src, dst, send, recv, device):
        return pltpu.make_async_remote_copy(
            src_ref=src, dst_ref=dst, send_sem=send, recv_sem=recv,
            device_id=device, device_id_type=pl.DeviceIdType.MESH,
        )

    halos = [
        (remote(rows_out.at[1], rows_lo, halo_send.at[0], halo_recv.at[0],
                {"cast": lax.rem(me + 1, n)}), me < n - 1, me > 0),
        (remote(rows_out.at[0], rows_hi, halo_send.at[1], halo_recv.at[1],
                {"cast": lax.rem(me + n - 1, n)}), me > 0, me < n - 1),
        (remote(cols_out, cols_lo, halo_send.at[2], halo_recv.at[2],
                {"width": lax.rem(mw + 1, nw)}), mw < nw - 1, mw > 0),
        (remote(cols_out, cols_hi, halo_send.at[3], halo_recv.at[3],
                {"width": lax.rem(mw + nw - 1, nw)}), mw > 0, mw < nw - 1),
    ]
    pl.semaphore_wait(barrier, n - 1 + nw - 1)
    for copy, sends, _ in halos:
        pl.when(sends)(copy.start)

    def properties(b, _):
        z = pl.ds(b * bz, bz)
        t, hot, cond = medium(x_ref[z])
        T[pl.ds(b * bz + 1, bz)] = hot
        K[pl.ds(b * bz + 1, bz)] = cond
        S[z] = 1.0 / ((1.0 - RELEASE) + RELEASE * t * t)
        U[z] = jnp.zeros((bz, rows, lanes), f32)
        for j, v in enumerate(by_rows(S, b * bz)):
            SX[b, j] = v
        return 0

    lax.fori_loop(0, nb, properties, 0)
    T[0], T[depth + 1] = T[1], T[depth]
    K[0], K[depth + 1] = -K[1], -K[depth]
    zones_copy.wait()
    for side, plane in ((0, 0), (1, depth - 1)):
        zone = zones_ref[side]
        coef = jnp.zeros((rows, lanes), f32)
        for i in range(coef_ref.shape[0]):
            coef = jnp.where(zone == i, coef_ref[i], coef)
        U[plane] = coef * (depth * depth / 8.0)

    for copy, _, receives in halos:
        pl.when(receives)(copy.wait_recv)

    gain_cast = rows * rows * 4.0 * 0.5
    gain_width = lanes * lanes / 4.0 * 0.5
    gain_thick = depth * depth / 4.0 * 0.5
    width_lo_mask = jnp.where(lane2 == 0, width_lo, 1.0)
    width_hi_mask = jnp.where(lane2 == lanes - 1, width_hi, 1.0)
    _, col_lo_T, col_lo_K = medium(cols_lo[...])
    _, col_hi_T, col_hi_K = medium(cols_hi[...])

    def gather_copy(dest):
        return remote(cs.at[dest], cr.at[me], a_send.at[dest], a_recv.at[me], {"cast": dest})

    def gather_wait(source):
        remote(cs.at[source], cr.at[source], a_send.at[source], a_recv.at[source],
               {"cast": source}).wait_recv()

    def cast_block(k, _):
        b = lax.rem(me // per + nb // 2 + k, nb)
        start = pl.multiple_of(b * bz, bz)
        hot, cond = by_rows(T, start + 1), by_rows(K, start + 1)
        hot_m, cond_m = by_rows(T, start), by_rows(K, start)
        hot_p, cond_p = by_rows(T, start + 2), by_rows(K, start + 2)
        surf = by_rows(U, start)
        _, hot_lo, cond_lo = medium(rows_lo[pl.ds(start, bz), :])
        _, hot_hi, cond_hi = medium(rows_hi[pl.ds(start, bz), :])
        hots, conds = [hot_lo] + hot + [hot_hi], [cond_lo] + cond + [cond_hi]
        faces = [gain_cast * (conds[j] + conds[j + 1]) for j in range(rows + 1)]
        faces[0], faces[rows] = faces[0] * cast_lo, faces[rows] * cast_hi
        flux = [faces[j] * (hots[j + 1] - hots[j]) for j in range(rows + 1)]

        lo_T, lo_K = spread(col_lo_T, b, 0), spread(col_lo_K, b, 0)
        hi_T, hi_K = spread(col_hi_T, b, 1), spread(col_hi_K, b, 1)
        r = []
        for j in range(rows):
            h, c = hot[j], cond[j]
            hm = jnp.where(lane2 == 0, lo_T[j], pltpu.roll(h, 1, 1))
            cm = jnp.where(lane2 == 0, lo_K[j], pltpu.roll(c, 1, 1))
            hp = jnp.where(lane2 == lanes - 1, hi_T[j], pltpu.roll(h, lanes - 1, 1))
            cp = jnp.where(lane2 == lanes - 1, hi_K[j], pltpu.roll(c, lanes - 1, 1))
            lo = gain_width * (c + cm) * width_lo_mask
            hi = gain_width * (c + cp) * width_hi_mask
            WL[b, j] = lo
            WR[b, j] = hi
            r.append(
                surf[j] * (MEDIUM - h)
                + (flux[j + 1] - flux[j])
                + (hi * (hp - h) - lo * (h - hm))
                + gain_thick
                * ((c + cond_p[j]) * (hot_p[j] - h) - (c + cond_m[j]) * (h - hot_m[j]))
            )
        s = [SX[b, j] for j in range(rows)]
        ys, ps, qs = row_levels(s, faces[1:rows], faces[0], faces[rows], r)
        for j in range(rows):
            Y[b, j] = ys[j]
            PP[b, j] = ps[j]
            Q[b, j] = qs[j]
        for o in range(per):
            dest = b * per + o
            for v, value in enumerate((ys[0], ps[0], qs[0], ys[-1], ps[-1], qs[-1])):
                cs[dest, v * pz : (v + 1) * pz] = value[o * pz : (o + 1) * pz]

            @pl.when(dest != me)
            def _():
                gather_copy(dest).start()

        return 0

    lax.fori_loop(0, nb, cast_block, 0)
    cr[me] = cs[me]

    def width_block(b, carry):
        lo, hi = WL[b], WR[b]
        left = jnp.where(lane3 == 0, lo, 0.0)
        right = jnp.where(lane3 == lanes - 1, hi, 0.0)
        ground, left, right, factors = lane_levels(
            SX[b] + left + right, lo - left, hi - right, left, right
        )
        for i, (al, ga) in enumerate(factors):
            AL[i, b] = al
            GA[i, b] = ga
        w = 1.0 / ground
        p, q = left * w, right * w
        WW[b], WP[b], WQ[b] = w, p, q
        return carry[0] + pack(p, b), carry[1] + pack(q, b)

    p_ends, q_ends = lax.fori_loop(0, nb, width_block, (zero, zero))
    wc[mw, 0] = p_ends
    wc[mw, 1] = q_ends
    wide_coefs = [
        remote(wc.at[mw], wc.at[mw], c_send.at[k - 1], c_recv.at[k - 1],
               {"width": lax.rem(mw + k, nw)})
        for k in range(1, nw)
    ]
    for copy in wide_coefs:
        copy.start()

    for i in range(n):
        pl.when(me != i)(functools.partial(gather_wait, i))
    got = [[cr[i, v * pz : (v + 1) * pz] for v in range(6)] for i in range(n)]
    a0, a1, a2, b0, b1, b2 = [[got[i][v] for i in range(n)] for v in range(6)]
    first, last = chain_values(a0, b0, a1, b1, chain_coefs(a1, a2, b1, b2))
    blank = jnp.zeros_like(first[0])

    def answer_copy(i):
        return remote(xs.at[i], xr.at[me], b_send.at[i], b_recv.at[me], {"cast": i})

    for i in range(n):
        xs[i, 0:pz] = last[i - 1] if i > 0 else blank
        xs[i, pz : 2 * pz] = first[i + 1] if i < n - 1 else blank
        pl.when(me != i)(answer_copy(i).start)
    xr[me] = xs[me]

    half = depth // 2
    zlo_sum, zhi_sum = S[0] + U[0], S[depth - 1] + U[depth - 1]
    for i in range(half - 1):
        j = depth - 1 - i
        glo, ghi = gain_thick * (K[i + 1] + K[i + 2]), gain_thick * (K[j] + K[j + 1])
        wlo, whi = 1.0 / (zlo_sum + glo), 1.0 / (zhi_sum + ghi)
        mlo, mhi = glo * wlo, ghi * whi
        M[i], M[j] = mlo, mhi
        V[i], V[j] = wlo, whi
        zlo_sum = S[i + 1] + mlo * zlo_sum
        zhi_sum = S[j - 1] + mhi * zhi_sum
    gmid = gain_thick * (K[half] + K[half + 1])
    det = 1.0 / (zlo_sum * zhi_sum + gmid * (zlo_sum + zhi_sum))
    V[half - 1] = (zhi_sum + gmid) * det
    V[half] = (zlo_sum + gmid) * det
    M[half] = gmid * det

    def step_block(k, carry):
        b = lax.rem(me // per + k, nb)
        los, his = [], []
        for o in range(per):
            owner = b * per + o

            @pl.when(owner != me)
            def _():
                remote(xs.at[owner], xr.at[owner], b_send.at[owner], b_recv.at[owner],
                       {"cast": owner}).wait_recv()

            los.append(xr[owner, 0:pz])
            his.append(xr[owner, pz : 2 * pz])
        lo = los[0] if per == 1 else jnp.concatenate(los, 0)
        hi = his[0] if per == 1 else jnp.concatenate(his, 0)
        r = (Y[b] + PP[b] * lo[None] + Q[b] * hi[None]) * SX[b]
        step, i = 1, 0
        while step < lanes:
            r = apply_level(r, AL[i, b], GA[i, b], step, 2)
            step, i = step * 2, i + 1
        r = r * WW[b]
        DX[b] = r
        return carry + pack(r, b)

    wv[mw] = lax.fori_loop(0, nb, step_block, zero)
    wide_values = [
        remote(wv.at[mw], wv.at[mw], d_send.at[k - 1], d_recv.at[k - 1],
               {"width": lax.rem(mw + k, nw)})
        for k in range(1, nw)
    ]
    for copy in wide_values:
        copy.start()

    for copy in wide_coefs:
        copy.wait_recv()

    def firsts(p):
        return pltpu.roll(p, lanes - 1, 1)

    even = lane2 % 2 == 0
    b1 = [jnp.where(even, wc[i, 0], 0.0) for i in range(nw)]
    b2 = [jnp.where(even, wc[i, 1], 0.0) for i in range(nw)]
    a1 = [jnp.where(even, firsts(wc[i, 0]), 0.0) for i in range(nw)]
    a2 = [jnp.where(even, firsts(wc[i, 1]), 0.0) for i in range(nw)]
    coefs = chain_coefs(a1, a2, b1, b2)
    for copy in wide_values:
        copy.wait_recv()
    b0 = [wv[i] for i in range(nw)]
    a0 = [firsts(b0[i]) for i in range(nw)]
    first, last = chain_values(a0, b0, a1, b1, coefs)
    before, after = zero, zero
    for i in range(nw):
        if i > 0:
            before = jnp.where(mw == i, last[i - 1], before)
        if i < nw - 1:
            after = jnp.where(mw == i, first[i + 1], after)

    def thick_block(b, _):
        start = b * bz
        los, his = spread(before, b, 0), spread(after, b, 0)
        for j in range(rows):
            D[pl.ds(start, bz), j, :] = (DX[b, j] + WP[b, j] * los[j] + WQ[b, j] * his[j]) * SX[
                b, j
            ]
        return 0

    lax.fori_loop(0, nb, thick_block, 0)

    dlo, dhi = D[0], D[depth - 1]
    for i in range(half - 1):
        j = depth - 1 - i
        D[i], D[j] = dlo, dhi
        dlo = D[i + 1] + M[i] * dlo
        dhi = D[j - 1] + M[j] * dhi
    ulo = V[half - 1] * dlo + M[half] * dhi
    uhi = V[half] * dhi + M[half] * dlo
    out_ref[half - 1] = ulo * S[half - 1]
    out_ref[half] = uhi * S[half]
    for i in range(half - 2, -1, -1):
        j = depth - 1 - i
        ulo = V[i] * D[i] + M[i] * ulo
        uhi = V[j] * D[j] + M[j] * uhi
        out_ref[i] = ulo * S[i]
        out_ref[j] = uhi * S[j]

    for copy, sends, _ in halos:
        pl.when(sends)(copy.wait_send)
    for i in range(n):
        pl.when(me != i)(gather_copy(i).wait_send)
    for i in range(n):
        pl.when(me != i)(answer_copy(i).wait_send)
    for copy in wide_coefs + wide_values:
        copy.wait_send()


def shards(n, nw, x, zones, spray_coef):
    depth, rows, lanes = x.shape
    pz = depth // n
    f32 = jnp.float32
    vmem = pltpu.VMEM
    bz = max(pz, rows)
    nb = depth // bz
    field = vmem((depth, rows, lanes), f32)
    blocks = vmem((nb, rows, bz, lanes), f32)
    padded = vmem((depth + 2, rows, lanes), f32)
    levels = vmem(((lanes - 1).bit_length(), nb, rows, bz, lanes), f32)
    edge = vmem((depth, lanes), f32)
    packed = vmem((bz, lanes), f32)
    dma = pltpu.SemaphoreType.DMA
    scratch = (
        [field, vmem(zones.shape, zones.dtype), padded, padded]
        + [field, field]
        + [blocks] * 6
        + [levels, levels]
        + [blocks] * 4
        + [field] * 3
        + [vmem((2, depth, lanes), f32), edge, edge, packed, packed, packed]
        + [
            vmem((n, 6 * pz, lanes), f32),
            vmem((n, 6 * pz, lanes), f32),
            vmem((n, 2 * pz, lanes), f32),
            vmem((n, 2 * pz, lanes), f32),
            vmem((nw, 2, bz, lanes), f32),
            vmem((nw, bz, lanes), f32),
        ]
        + [dma((2,)), dma((4,)), dma((4,))]
        + [dma((n,))] * 4
        + [dma((nw,))] * 4
    )
    step = pl.pallas_call(
        functools.partial(kernel, n, nw),
        out_shape=jax.ShapeDtypeStruct(x.shape, f32),
        in_specs=[
            pl.BlockSpec(memory_space=pl.ANY),
            pl.BlockSpec(memory_space=pl.ANY),
            pl.BlockSpec(memory_space=pltpu.SMEM),
        ],
        out_specs=pl.BlockSpec(memory_space=pltpu.VMEM),
        scratch_shapes=scratch,
        compiler_params=pltpu.CompilerParams(
            collective_id=0, has_side_effects=True, vmem_limit_bytes=32 * 1024 * 1024
        ),
        cost_estimate=pl.CostEstimate(
            flops=20_000_000, bytes_accessed=1_000_000, transcendentals=100_000
        ),
        name="adi_step",
    )(x, zones, spray_coef)
    return x + step


def solution(mesh):
    spec = P(None, "cast", "width")
    body = functools.partial(shards, mesh.shape["cast"], mesh.shape["width"])
    return jax.shard_map(
        body, mesh=mesh, in_specs=(spec, spec, P()), out_specs=spec, check_vma=False
    )
```

profile of v0, /device:TPU:0, one launch (start us, length us, event | category | flops | bytes accessed | tf_op | source)
XLA Modules:
  0.0 36.0 jit_solution(16385295182870619222)
XLA Ops:
  0.0 0.0 copy-start
  0.0 0.9 %copy-done = f32[64,8,128]{2,1,0:T(8,128)S(1)} copy-done((f32[64,8,128]{2,1,0:T(8,128)S(1)}, f32[64,8,128]{2,1,0:T(8,128)}, u32[]{:S(2)}) %copy-start) | copy-done | bytes 262168
  1.0 0.0 copy-start.1
  1.0 0.7 %copy-done.1 = s32[2,8,128]{2,1,0:T(8,128)S(1)} copy-done((s32[2,8,128]{2,1,0:T(8,128)S(1)}, s32[2,8,128]{2,1,0:T(8,128)}, u32[]{:S(2)}) %copy-start.1) | copy-done | bytes 8216
  1.6 0.0 copy-start.2
  1.7 0.7 %copy-done.2 = f32[10]{0:T(128)S(1)} copy-done((f32[10]{0:T(128)S(1)}, f32[10]{0:T(128)}, u32[]{:S(2)}) %copy-start.2) | copy-done | bytes 64
  2.3 32.9 %adi_step.1 = f32[64,8,128]{2,1,0:T(8,128)S(1)} custom-call(f32[64,8,128]{2,1,0:T(8,128)S(1)} %copy-done, s32[2,8,128]{2,1,0:T(8,128)S(1)} %copy-done.1, f32[10]{0:T(128)S(1)} %copy-done.2), custom_call_target="tpu_custom_call" | custom-call | flops 20000000 | bytes 1000000 | tf_op jit(solution)/shard_map/adi_step/pallas_call | solution.py:514
  35.3 0.7 %add.3 = f32[64,8,128]{2,1,0:T(8,128)} add(f32[64,8,128]{2,1,0:T(8,128)S(1)} %copy-done, f32[64,8,128]{2,1,0:T(8,128)S(1)} %adi_step.1) | non-fusion elementwise | flops 65536 | bytes 786432 | tf_op jit(solution)/shard_map/add | solution.py:532
Async XLA Ops:
  0.0 0.9 %copy-start = (f32[64,8,128]{2,1,0:T(8,128)S(1)}, f32[64,8,128]{2,1,0:T(8,128)}, u32[]{:S(2)}) copy-start(f32[64,8,128]{2,1,0:T(8,128)} %x_hbm.1) | copy-start | bytes 786436
  1.0 0.7 %copy-start.1 = (s32[2,8,128]{2,1,0:T(8,128)S(1)}, s32[2,8,128]{2,1,0:T(8,128)}, u32[]{:S(2)}) copy-start(s32[2,8,128]{2,1,0:T(8,128)} %zones_hbm.1) | copy-start | bytes 24580
  1.6 0.7 %copy-start.2 = (f32[10]{0:T(128)S(1)}, f32[10]{0:T(128)}, u32[]{:S(2)}) copy-start(f32[10]{0:T(128)} %coef_ref.1) | copy-start | bytes 124
where the time goes:
time: 36.2 us; the launch traced here: 36 us
  Pallas kernels  32.9 us (91%)
  local copies, waits for them, and re-layouts  2.3 us (6%)
  other arithmetic  0.73 us (2%)
    pallas_call x1, Pallas kernels, shards(): pl.pallas_call(functools.partial(kernel, n, nw), out_shape=jax.ShapeDtype...  32.9 us
    unnamed x6, local copies, waits for them, and re-layouts  2.3 us
    add x1, other arithmetic, shards(): return x + step  0.73 us

commit v1 on v0

--- a/solution.py
+++ b/solution.py
@@ -136,8 +136,8 @@
 
 
 def kernel(
-    n, nw, x_hbm, zones_hbm, coef_ref, out_ref,
-    x_ref, zones_ref, T, K, S, U, SX, WL, WR, Y, PP, Q, AL, GA, WW, WP, WQ, DX, D, M, V,
+    n, nw, x_hbm, zones_hbm, coef_hbm, out_ref,
+    coef_ref, x_ref, zones_ref, T, K, S, U, SX, WL, WR, Y, PP, Q, AL, GA, WW, WP, WQ, DX, D, M, V,
     rows_out, rows_lo, rows_hi, cols_out, cols_lo, cols_hi,
     cs, cr, xs, xr, wc, wv,
     in_sem, halo_send, halo_recv, a_send, a_recv, b_send, b_recv, c_send, c_recv, d_send, d_recv,
@@ -153,8 +153,10 @@
 
     x_copy = pltpu.make_async_copy(x_hbm, x_ref, in_sem.at[0])
     zones_copy = pltpu.make_async_copy(zones_hbm, zones_ref, in_sem.at[1])
+    coef_copy = pltpu.make_async_copy(coef_hbm, coef_ref, in_sem.at[2])
     x_copy.start()
     zones_copy.start()
+    coef_copy.start()
 
     barrier = pltpu.get_barrier_semaphore()
     for k in range(1, n):
@@ -244,6 +246,7 @@
     T[0], T[depth + 1] = T[1], T[depth]
     K[0], K[depth + 1] = -K[1], -K[depth]
     zones_copy.wait()
+    coef_copy.wait()
     for side, plane in ((0, 0), (1, depth - 1)):
         zone = zones_ref[side]
         coef = jnp.zeros((rows, lanes), f32)
@@ -482,7 +485,7 @@
     pz = depth // n
     f32 = jnp.float32
     vmem = pltpu.VMEM
-    bz = max(pz, rows)
+    bz = max(pz, depth // 2)
     nb = depth // bz
     field = vmem((depth, rows, lanes), f32)
     blocks = vmem((nb, rows, bz, lanes), f32)
@@ -492,7 +495,8 @@
     packed = vmem((bz, lanes), f32)
     dma = pltpu.SemaphoreType.DMA
     scratch = (
-        [field, vmem(zones.shape, zones.dtype), padded, padded]
+        [pltpu.SMEM(spray_coef.shape, f32)]
+        + [field, vmem(zones.shape, zones.dtype), padded, padded]
         + [field, field]
         + [blocks] * 6
         + [levels, levels]
@@ -507,7 +511,7 @@
             vmem((nw, 2, bz, lanes), f32),
             vmem((nw, bz, lanes), f32),
         ]
-        + [dma((2,)), dma((4,)), dma((4,))]
+        + [dma((3,)), dma((4,)), dma((4,))]
         + [dma((n,))] * 4
         + [dma((nw,))] * 4
     )
@@ -515,14 +519,14 @@
         functools.partial(kernel, n, nw),
         out_shape=jax.ShapeDtypeStruct(x.shape, f32),
         in_specs=[
-            pl.BlockSpec(memory_space=pl.ANY),
-            pl.BlockSpec(memory_space=pl.ANY),
-            pl.BlockSpec(memory_space=pltpu.SMEM),
+            pl.BlockSpec(memory_space=pltpu.HBM),
+            pl.BlockSpec(memory_space=pltpu.HBM),
+            pl.BlockSpec(memory_space=pltpu.HBM),
         ],
         out_specs=pl.BlockSpec(memory_space=pltpu.VMEM),
         scratch_shapes=scratch,
         compiler_params=pltpu.CompilerParams(
-            collective_id=0, has_side_effects=True, vmem_limit_bytes=32 * 1024 * 1024
+            collective_id=0, has_side_effects=True, vmem_limit_bytes=63 * 1024 * 1024
         ),
         cost_estimate=pl.CostEstimate(
             flops=20_000_000, bytes_accessed=1_000_000, transcendentals=100_000

time: 36.2 us -> 28.9 us (0.80)
  Pallas kernels: 32.9 us -> 27 us
  local copies, waits for them, and re-layouts: 2.3 us -> 0.01 us
  other arithmetic: 0.73 us -> 1.68 us
    pallas_call x1, Pallas kernels: 32.9 us -> 27 us  [shards(): pl.pallas_call(functools.partial(kernel, n, nw), out_shape=jax.ShapeDtype...]
    unnamed x6 -> x2, local copies, waits for them, and re-layouts: 2.3 us -> 0.01 us
    add x1, other arithmetic: 0.73 us -> 1.68 us  [shards(): return x + step]
where the time goes in v1:
time: 28.9 us; the launch traced here: 28.7 us
  Pallas kernels  27 us (93%)
  other arithmetic  1.68 us (6%)
    pallas_call x1, Pallas kernels, shards(): pl.pallas_call(functools.partial(kernel, n, nw), out_shape=jax.ShapeDtype...  27 us
    add x1, other arithmetic, shards(): return x + step  1.68 us

profile of v1, /device:TPU:0, one launch (start us, length us, event | category | flops | bytes accessed | tf_op | source)
XLA Modules:
  0.0 28.7 jit_solution(9174463394916466312)
XLA Ops:
  0.0 0.0 copy-start
  0.0 27.0 %adi_step.1 = f32[64,8,128]{2,1,0:T(8,128)} custom-call(f32[64,8,128]{2,1,0:T(8,128)} %x_hbm.1, s32[2,8,128]{2,1,0:T(8,128)} %zones_hbm.1, f32[10]{0:T(128)} %coef_hbm.1), custom_call_target="tpu_custom_call" | custom-call | flops 20000000 | bytes 1000000 | tf_op jit(solution)/shard_map/adi_step/pallas_call | solution.py:518
  27.0 0.0 copy-done
  27.1 1.7 %add.3 = f32[64,8,128]{2,1,0:T(8,128)} add(f32[64,8,128]{2,1,0:T(8,128)S(1)} %copy-done, f32[64,8,128]{2,1,0:T(8,128)} %adi_step.1) | non-fusion elementwise | flops 65536 | bytes 786432 | tf_op jit(solution)/shard_map/add | solution.py:536
Async XLA Ops:
  0.0 27.1 %copy-start = (f32[64,8,128]{2,1,0:T(8,128)S(1)}, f32[64,8,128]{2,1,0:T(8,128)}, u32[]{:S(2)}) copy-start(f32[64,8,128]{2,1,0:T(8,128)} %x_hbm.1) | copy-start | bytes 786436

commit v2 on v1

--- a/solution.py
+++ b/solution.py
@@ -95,44 +95,54 @@
     return r + al * pltpu.roll(r, step, axis) + ga * pltpu.roll(r, size - step, axis)
 
 
+def half_coefs(a1, a2, b1, b2):
+    out = [(None, None, a2[0], b2[0])]
+    for i in range(1, len(a1)):
+        e1 = out[-1][3]
+        c = 1.0 / (1.0 - a1[i] * e1)
+        be = b1[i] * e1
+        f2 = c * a2[i]
+        out.append((c, be, f2, be * f2 + b2[i]))
+    return out
+
+
+def half_values(a0, b0, a1, b1, coefs):
+    out = [(a0[0], b0[0])]
+    for i in range(1, len(a0)):
+        c, be, _, _ = coefs[i]
+        e0 = out[-1][1]
+        f0 = c * (a0[i] + a1[i] * e0)
+        out.append((f0, b0[i] + b1[i] * e0 + be * f0))
+    return out
+
+
+def half_back(values, coefs, beyond):
+    first, last = [], []
+    for (f0, e0), (_, _, f2, e1) in zip(reversed(values), reversed(coefs)):
+        last.append(e0 + e1 * beyond)
+        beyond = f0 + f2 * beyond
+        first.append(beyond)
+    return first[::-1], last[::-1]
+
+
 def chain_coefs(a1, a2, b1, b2):
-    out = []
-    e1 = None
-    for i in range(len(a1)):
-        if e1 is None:
-            c, be = None, None
-            f2 = a2[i]
-            e1 = b2[i]
-        else:
-            c = 1.0 / (1.0 - a1[i] * e1)
-            be = b1[i] * e1
-            f2 = c * a2[i]
-            e1 = be * f2 + b2[i]
-        out.append((c, be, f2, e1))
-    return out
-
-
-def chain_values(a0, b0, a1, b1, coefs):
-    n = len(a0)
-    f0s, e0s = [], []
-    e0 = None
-    for i in range(n):
-        c, be, f2, e1 = coefs[i]
-        if e0 is None:
-            f0 = a0[i]
-            e0 = b0[i]
-        else:
-            f0 = c * (a0[i] + a1[i] * e0)
-            e0 = b0[i] + b1[i] * e0 + be * f0
-        f0s.append(f0)
-        e0s.append(e0)
-    first, last = [None] * n, [None] * n
-    first[n - 1], last[n - 1] = f0s[n - 1], e0s[n - 1]
-    for i in range(n - 2, -1, -1):
-        _, _, f2, e1 = coefs[i]
-        first[i] = f0s[i] + f2 * first[i + 1]
-        last[i] = e0s[i] + e1 * first[i + 1]
-    return first, last
+    m = len(a1) // 2
+    low = half_coefs(a1[:m], a2[:m], b1[:m], b2[:m])
+    high = half_coefs(b2[m:][::-1], b1[m:][::-1], a2[m:][::-1], a1[m:][::-1])
+    return low, high, 1.0 / (1.0 - low[-1][3] * high[-1][3])
+
+
+def chain_values(a0, b0, a1, a2, b1, b2, coefs):
+    m = len(a0) // 2
+    low, high, c = coefs
+    low_values = half_values(a0[:m], b0[:m], a1[:m], b1[:m], low)
+    high_values = half_values(b0[m:][::-1], a0[m:][::-1], b2[m:][::-1], a2[m:][::-1], high)
+    low_end, high_end = low_values[-1][1], high_values[-1][1]
+    end = c * (low_end + low[-1][3] * high_end)
+    start = high_end + high[-1][3] * end
+    first, last = half_back(low_values, low, start)
+    last_high, first_high = half_back(high_values, high, end)
+    return first + first_high[::-1], last + last_high[::-1]
 
 
 def kernel(
@@ -165,7 +175,6 @@
         pl.semaphore_signal(barrier, inc=1, device_id={"width": lax.rem(mw + k, nw)})
 
     lane2 = lax.broadcasted_iota(jnp.int32, (bz, lanes), 1)
-    lane3 = lax.broadcasted_iota(jnp.int32, (rows, bz, lanes), 2)
     zero = jnp.zeros((bz, lanes), f32)
     cast_lo = (me > 0).astype(f32)
     cast_hi = (me < n - 1).astype(f32)
@@ -176,7 +185,7 @@
         acc = zero
         for j in range(rows):
             acc = jnp.where(lane2 // 2 == j, pltpu.roll(v[j], 2 * j + 1, 1), acc)
-        return pltpu.roll(acc, b * (2 * rows), 1)
+        return acc if isinstance(b, int) and b == 0 else pltpu.roll(acc, b * (2 * rows), 1)
 
     def spread(p, b, odd):
         q = pltpu.roll(p, lax.rem(lanes - b * (2 * rows), lanes), 1)
@@ -326,22 +335,21 @@
     lax.fori_loop(0, nb, cast_block, 0)
     cr[me] = cs[me]
 
-    def width_block(b, carry):
-        lo, hi = WL[b], WR[b]
-        left = jnp.where(lane3 == 0, lo, 0.0)
-        right = jnp.where(lane3 == lanes - 1, hi, 0.0)
-        ground, left, right, factors = lane_levels(
-            SX[b] + left + right, lo - left, hi - right, left, right
-        )
-        for i, (al, ga) in enumerate(factors):
-            AL[i, b] = al
-            GA[i, b] = ga
-        w = 1.0 / ground
-        p, q = left * w, right * w
-        WW[b], WP[b], WQ[b] = w, p, q
-        return carry[0] + pack(p, b), carry[1] + pack(q, b)
-
-    p_ends, q_ends = lax.fori_loop(0, nb, width_block, (zero, zero))
+    lane4 = lax.broadcasted_iota(jnp.int32, SX.shape, 3)
+    lo, hi = WL[...], WR[...]
+    left = jnp.where(lane4 == 0, lo, 0.0)
+    right = jnp.where(lane4 == lanes - 1, hi, 0.0)
+    ground, left, right, factors = lane_levels(
+        SX[...] + left + right, lo - left, hi - right, left, right
+    )
+    for i, (al, ga) in enumerate(factors):
+        AL[i] = al
+        GA[i] = ga
+    w = 1.0 / ground
+    p, q = left * w, right * w
+    WW[...], WP[...], WQ[...] = w, p, q
+    p_ends = sum(pack(p[b], b) for b in range(nb))
+    q_ends = sum(pack(q[b], b) for b in range(nb))
     wc[mw, 0] = p_ends
     wc[mw, 1] = q_ends
     wide_coefs = [
@@ -356,7 +364,9 @@
         pl.when(me != i)(functools.partial(gather_wait, i))
     got = [[cr[i, v * pz : (v + 1) * pz] for v in range(6)] for i in range(n)]
     a0, a1, a2, b0, b1, b2 = [[got[i][v] for i in range(n)] for v in range(6)]
-    first, last = chain_values(a0, b0, a1, b1, chain_coefs(a1, a2, b1, b2))
+    first, last = chain_values(
+        a0, b0, a1, a2, b1, b2, chain_coefs(a1, a2, b1, b2)
+    )
     blank = jnp.zeros_like(first[0])
 
     def answer_copy(i):
@@ -385,31 +395,21 @@
     V[half] = (zlo_sum + gmid) * det
     M[half] = gmid * det
 
-    def step_block(k, carry):
-        b = lax.rem(me // per + k, nb)
-        los, his = [], []
-        for o in range(per):
-            owner = b * per + o
-
-            @pl.when(owner != me)
-            def _():
-                remote(xs.at[owner], xr.at[owner], b_send.at[owner], b_recv.at[owner],
-                       {"cast": owner}).wait_recv()
-
-            los.append(xr[owner, 0:pz])
-            his.append(xr[owner, pz : 2 * pz])
-        lo = los[0] if per == 1 else jnp.concatenate(los, 0)
-        hi = his[0] if per == 1 else jnp.concatenate(his, 0)
-        r = (Y[b] + PP[b] * lo[None] + Q[b] * hi[None]) * SX[b]
-        step, i = 1, 0
-        while step < lanes:
-            r = apply_level(r, AL[i, b], GA[i, b], step, 2)
-            step, i = step * 2, i + 1
-        r = r * WW[b]
-        DX[b] = r
-        return carry + pack(r, b)
-
-    wv[mw] = lax.fori_loop(0, nb, step_block, zero)
+    def answer_wait(i):
+        remote(xs.at[i], xr.at[i], b_send.at[i], b_recv.at[i], {"cast": i}).wait_recv()
+
+    for i in range(n):
+        pl.when(me != i)(functools.partial(answer_wait, i))
+    los = jnp.concatenate([xr[i, 0:pz] for i in range(n)], 0).reshape(nb, 1, bz, lanes)
+    his = jnp.concatenate([xr[i, pz : 2 * pz] for i in range(n)], 0).reshape(nb, 1, bz, lanes)
+    r = (Y[...] + PP[...] * los + Q[...] * his) * SX[...]
+    step, i = 1, 0
+    while step < lanes:
+        r = apply_level(r, AL[i], GA[i], step, 3)
+        step, i = step * 2, i + 1
+    r = r * WW[...]
+    DX[...] = r
+    wv[mw] = sum(pack(r[b], b) for b in range(nb))
     wide_values = [
         remote(wv.at[mw], wv.at[mw], d_send.at[k - 1], d_recv.at[k - 1],
                {"width": lax.rem(mw + k, nw)})
@@ -434,7 +434,7 @@
         copy.wait_recv()
     b0 = [wv[i] for i in range(nw)]
     a0 = [firsts(b0[i]) for i in range(nw)]
-    first, last = chain_values(a0, b0, a1, b1, coefs)
+    first, last = chain_values(a0, b0, a1, a2, b1, b2, coefs)
     before, after = zero, zero
     for i in range(nw):
         if i > 0:

time: 28.9 us -> 28.5 us (0.986)
  Pallas kernels: 27 us -> 26.7 us
    pallas_call x1, Pallas kernels: 27 us -> 26.7 us  [shards(): pl.pallas_call(functools.partial(kernel, n, nw), out_shape=jax.ShapeDtype...]
where the time goes in v2:
time: 28.5 us; the launch traced here: 28.4 us
  Pallas kernels  26.7 us (94%)
  other arithmetic  1.68 us (6%)
    pallas_call x1, Pallas kernels, shards(): pl.pallas_call(functools.partial(kernel, n, nw), out_shape=jax.ShapeDtype...  26.7 us
    add x1, other arithmetic, shards(): return x + step  1.68 us

profile of v2, /device:TPU:0, one launch (start us, length us, event | category | flops | bytes accessed | tf_op | source)
XLA Modules:
  0.0 28.4 jit_solution(1478325912762671993)
XLA Ops:
  0.0 0.0 copy-start
  0.0 26.7 %adi_step.1 = f32[64,8,128]{2,1,0:T(8,128)} custom-call(f32[64,8,128]{2,1,0:T(8,128)} %x_hbm.1, s32[2,8,128]{2,1,0:T(8,128)} %zones_hbm.1, f32[10]{0:T(128)} %coef_hbm.1), custom_call_target="tpu_custom_call" | custom-call | flops 20000000 | bytes 1000000 | tf_op jit(solution)/shard_map/adi_step/pallas_call | solution.py:518
  26.7 0.0 copy-done
  26.7 1.7 %add.3 = f32[64,8,128]{2,1,0:T(8,128)} add(f32[64,8,128]{2,1,0:T(8,128)S(1)} %copy-done, f32[64,8,128]{2,1,0:T(8,128)} %adi_step.1) | non-fusion elementwise | flops 65536 | bytes 786432 | tf_op jit(solution)/shard_map/add | solution.py:536
Async XLA Ops:
  0.0 26.7 %copy-start = (f32[64,8,128]{2,1,0:T(8,128)S(1)}, f32[64,8,128]{2,1,0:T(8,128)}, u32[]{:S(2)}) copy-start(f32[64,8,128]{2,1,0:T(8,128)} %x_hbm.1) | copy-start | bytes 786436

commit v3 on v2

--- a/solution.py
+++ b/solution.py
@@ -148,7 +148,7 @@
 def kernel(
     n, nw, x_hbm, zones_hbm, coef_hbm, out_ref,
     coef_ref, x_ref, zones_ref, T, K, S, U, SX, WL, WR, Y, PP, Q, AL, GA, WW, WP, WQ, DX, D, M, V,
-    rows_out, rows_lo, rows_hi, cols_out, cols_lo, cols_hi,
+    RL, RH, rows_out, rows_lo, rows_hi, cols_out, cols_lo, cols_hi,
     cs, cr, xs, xr, wc, wv,
     in_sem, halo_send, halo_recv, a_send, a_recv, b_send, b_recv, c_send, c_recv, d_send, d_recv,
 ):
@@ -292,6 +292,9 @@
         _, hot_hi, cond_hi = medium(rows_hi[pl.ds(start, bz), :])
         hots, conds = [hot_lo] + hot + [hot_hi], [cond_lo] + cond + [cond_hi]
         faces = [gain_cast * (conds[j] + conds[j + 1]) for j in range(rows + 1)]
+        root_lo, root_hi = jnp.sqrt(faces[0]), jnp.sqrt(faces[rows])
+        inv_lo, inv_hi = 1.0 / root_lo, 1.0 / root_hi
+        RL[b], RH[b] = inv_lo, inv_hi
         faces[0], faces[rows] = faces[0] * cast_lo, faces[rows] * cast_hi
         flux = [faces[j] * (hots[j + 1] - hots[j]) for j in range(rows + 1)]
 
@@ -321,9 +324,13 @@
             Y[b, j] = ys[j]
             PP[b, j] = ps[j]
             Q[b, j] = qs[j]
+        cross = jnp.where(
+            me == n - 1, ps[-1] * (root_hi * inv_lo), qs[0] * (root_lo * inv_hi)
+        )
+        sent = (ys[0] * root_lo, ps[0], cross, ys[-1] * root_hi, qs[-1])
         for o in range(per):
             dest = b * per + o
-            for v, value in enumerate((ys[0], ps[0], qs[0], ys[-1], ps[-1], qs[-1])):
+            for v, value in enumerate(sent):
                 cs[dest, v * pz : (v + 1) * pz] = value[o * pz : (o + 1) * pz]
 
             @pl.when(dest != me)
@@ -362,8 +369,9 @@
 
     for i in range(n):
         pl.when(me != i)(functools.partial(gather_wait, i))
-    got = [[cr[i, v * pz : (v + 1) * pz] for v in range(6)] for i in range(n)]
-    a0, a1, a2, b0, b1, b2 = [[got[i][v] for i in range(n)] for v in range(6)]
+    got = [[cr[i, v * pz : (v + 1) * pz] for v in range(5)] for i in range(n)]
+    a0, a1, a2, b0, b2 = [[got[i][v] for i in range(n)] for v in range(5)]
+    b1 = a2
     first, last = chain_values(
         a0, b0, a1, a2, b1, b2, chain_coefs(a1, a2, b1, b2)
     )
@@ -400,8 +408,9 @@
 
     for i in range(n):
         pl.when(me != i)(functools.partial(answer_wait, i))
-    los = jnp.concatenate([xr[i, 0:pz] for i in range(n)], 0).reshape(nb, 1, bz, lanes)
-    his = jnp.concatenate([xr[i, pz : 2 * pz] for i in range(n)], 0).reshape(nb, 1, bz, lanes)
+    los = jnp.concatenate([xr[i, 0:pz] for i in range(n)], 0).reshape(nb, bz, lanes)
+    his = jnp.concatenate([xr[i, pz : 2 * pz] for i in range(n)], 0).reshape(nb, bz, lanes)
+    los, his = (los * RL[...])[:, None], (his * RH[...])[:, None]
     r = (Y[...] + PP[...] * los + Q[...] * his) * SX[...]
     step, i = 1, 0
     while step < lanes:
@@ -502,10 +511,11 @@
         + [levels, levels]
         + [blocks] * 4
         + [field] * 3
+        + [vmem((nb, bz, lanes), f32)] * 2
         + [vmem((2, depth, lanes), f32), edge, edge, packed, packed, packed]
         + [
-            vmem((n, 6 * pz, lanes), f32),
-            vmem((n, 6 * pz, lanes), f32),
+            vmem((n, 5 * pz, lanes), f32),
+            vmem((n, 5 * pz, lanes), f32),
             vmem((n, 2 * pz, lanes), f32),
             vmem((n, 2 * pz, lanes), f32),
             vmem((nw, 2, bz, lanes), f32),

time: 28.5 us -> 28.2 us (0.989)
  Pallas kernels: 26.7 us -> 26.3 us
    pallas_call x1, Pallas kernels: 26.7 us -> 26.3 us  [shards(): pl.pallas_call(functools.partial(kernel, n, nw), out_shape=jax.ShapeDtype...]
where the time goes in v3:
time: 28.2 us; the launch traced here: 28 us
  Pallas kernels  26.3 us (93%)
  other arithmetic  1.68 us (6%)
    pallas_call x1, Pallas kernels, shards(): pl.pallas_call(functools.partial(kernel, n, nw), out_shape=jax.ShapeDtype...  26.3 us
    add x1, other arithmetic, shards(): return x + step  1.68 us

profile of v3, /device:TPU:0, one launch (start us, length us, event | category | flops | bytes accessed | tf_op | source)
XLA Modules:
  0.0 28.0 jit_solution(6474353611808587314)
XLA Ops:
  0.0 0.0 copy-start
  0.0 26.3 %adi_step.1 = f32[64,8,128]{2,1,0:T(8,128)} custom-call(f32[64,8,128]{2,1,0:T(8,128)} %x_hbm.1, s32[2,8,128]{2,1,0:T(8,128)} %zones_hbm.1, f32[10]{0:T(128)} %coef_hbm.1), custom_call_target="tpu_custom_call" | custom-call | flops 20000000 | bytes 1000000 | tf_op jit(solution)/shard_map/adi_step/pallas_call | solution.py:528
  26.3 0.0 copy-done
  26.3 1.7 %add.3 = f32[64,8,128]{2,1,0:T(8,128)} add(f32[64,8,128]{2,1,0:T(8,128)S(1)} %copy-done, f32[64,8,128]{2,1,0:T(8,128)} %adi_step.1) | non-fusion elementwise | flops 65536 | bytes 786432 | tf_op jit(solution)/shard_map/add | solution.py:546
Async XLA Ops:
  0.0 26.3 %copy-start = (f32[64,8,128]{2,1,0:T(8,128)S(1)}, f32[64,8,128]{2,1,0:T(8,128)}, u32[]{:S(2)}) copy-start(f32[64,8,128]{2,1,0:T(8,128)} %x_hbm.1) | copy-start | bytes 786436

commit v4 on v3

--- a/solution.py
+++ b/solution.py
@@ -147,10 +147,10 @@
 
 def kernel(
     n, nw, x_hbm, zones_hbm, coef_hbm, out_ref,
-    coef_ref, x_ref, zones_ref, T, K, S, U, SX, WL, WR, Y, PP, Q, AL, GA, WW, WP, WQ, DX, D, M, V,
+    coef_ref, x_ref, zones_ref, T, K, S, U, SX, WL, WR, Y, PP, Q, AL, GA, WW, WP, WQ, DX, D, M, V, O,
     RL, RH, rows_out, rows_lo, rows_hi, cols_out, cols_lo, cols_hi,
     cs, cr, xs, xr, wc, wv,
-    in_sem, halo_send, halo_recv, a_send, a_recv, b_send, b_recv, c_send, c_recv, d_send, d_recv,
+    in_sem, out_sem, halo_send, halo_recv, a_send, a_recv, b_send, b_recv, c_send, c_recv, d_send, d_recv,
 ):
     depth, rows, lanes = x_ref.shape
     pz = depth // n
@@ -470,14 +470,25 @@
         dhi = D[j - 1] + M[j] * dhi
     ulo = V[half - 1] * dlo + M[half] * dhi
     uhi = V[half] * dhi + M[half] * dlo
-    out_ref[half - 1] = ulo * S[half - 1]
-    out_ref[half] = uhi * S[half]
+    O[half - 1] = ulo * S[half - 1]
+    O[half] = uhi * S[half]
+    part = half // 4
+    out_copies = []
     for i in range(half - 2, -1, -1):
         j = depth - 1 - i
         ulo = V[i] * D[i] + M[i] * ulo
         uhi = V[j] * D[j] + M[j] * uhi
-        out_ref[i] = ulo * S[i]
-        out_ref[j] = uhi * S[j]
+        O[i] = ulo * S[i]
+        O[j] = uhi * S[j]
+        if i % part == 0:
+            for start in (i, j + 1 - part):
+                planes = pl.ds(start, part)
+                out_copies.append(
+                    pltpu.make_async_copy(
+                        O.at[planes], out_ref.at[planes], out_sem.at[len(out_copies)]
+                    )
+                )
+                out_copies[-1].start()
 
     for copy, sends, _ in halos:
         pl.when(sends)(copy.wait_send)
@@ -487,6 +498,8 @@
         pl.when(me != i)(answer_copy(i).wait_send)
     for copy in wide_coefs + wide_values:
         copy.wait_send()
+    for copy in out_copies:
+        copy.wait()
 
 
 def shards(n, nw, x, zones, spray_coef):
@@ -510,7 +523,7 @@
         + [blocks] * 6
         + [levels, levels]
         + [blocks] * 4
-        + [field] * 3
+        + [field] * 4
         + [vmem((nb, bz, lanes), f32)] * 2
         + [vmem((2, depth, lanes), f32), edge, edge, packed, packed, packed]
         + [
@@ -521,7 +534,7 @@
             vmem((nw, 2, bz, lanes), f32),
             vmem((nw, bz, lanes), f32),
         ]
-        + [dma((3,)), dma((4,)), dma((4,))]
+        + [dma((3,)), dma((8,)), dma((4,)), dma((4,))]
         + [dma((n,))] * 4
         + [dma((nw,))] * 4
     )
@@ -533,7 +546,7 @@
             pl.BlockSpec(memory_space=pltpu.HBM),
             pl.BlockSpec(memory_space=pltpu.HBM),
         ],
-        out_specs=pl.BlockSpec(memory_space=pltpu.VMEM),
+        out_specs=pl.BlockSpec(memory_space=pltpu.HBM),
         scratch_shapes=scratch,
         compiler_params=pltpu.CompilerParams(
             collective_id=0, has_side_effects=True, vmem_limit_bytes=63 * 1024 * 1024

time: 28.2 us -> 28.2 us (level)
  no operation moved by 1% of the time
where the time goes in v4:
time: 28.2 us; the launch traced here: 28 us
  Pallas kernels  26.3 us (93%)
  other arithmetic  1.68 us (6%)
    pallas_call x1, Pallas kernels, shards(): pl.pallas_call(functools.partial(kernel, n, nw), out_shape=jax.ShapeDtype...  26.3 us
    add x1, other arithmetic, shards(): return x + step  1.68 us

profile of v4, /device:TPU:0, one launch (start us, length us, event | category | flops | bytes accessed | tf_op | source)
XLA Modules:
  0.0 28.0 jit_solution(13164350120942882317)
XLA Ops:
  0.0 0.0 copy-start
  0.0 26.3 %adi_step.1 = f32[64,8,128]{2,1,0:T(8,128)} custom-call(f32[64,8,128]{2,1,0:T(8,128)} %x_hbm.1, s32[2,8,128]{2,1,0:T(8,128)} %zones_hbm.1, f32[10]{0:T(128)} %coef_hbm.1), custom_call_target="tpu_custom_call" | custom-call | flops 20000000 | bytes 1000000 | tf_op jit(solution)/shard_map/adi_step/pallas_call | solution.py:541
  26.3 0.0 copy-done
  26.3 1.7 %add.3 = f32[64,8,128]{2,1,0:T(8,128)} add(f32[64,8,128]{2,1,0:T(8,128)S(1)} %copy-done, f32[64,8,128]{2,1,0:T(8,128)} %adi_step.1) | non-fusion elementwise | flops 65536 | bytes 786432 | tf_op jit(solution)/shard_map/add | solution.py:559
Async XLA Ops:
  0.0 26.3 %copy-start = (f32[64,8,128]{2,1,0:T(8,128)S(1)}, f32[64,8,128]{2,1,0:T(8,128)}, u32[]{:S(2)}) copy-start(f32[64,8,128]{2,1,0:T(8,128)} %x_hbm.1) | copy-start | bytes 786436
